TPU v7x, 32 devices: a whole 2x2x4 slice. The times are simulated.
32 devices in a mesh: seq: 4 (over z), head: 2 (over core), dp: 4 (over y, x).
Axes of the slice: x: 2, y: 2, z: 4, core: 2. Of those that a mesh axis runs over, the one named last changes fastest.
Arguments:
- series: bfloat16 [4, 2048, 768], P('dp', 'seq'), may hold values from -6 to 6
- norm_attn: float32 [768], replicated, may hold values from 0.1 to 1.9
- qkv_weight: bfloat16 [768, 3, 768], P(None, None, 'head'), may hold values from -0.21875 to 0.21875
- out_weight: bfloat16 [768, 768], P('head'), may hold values from -0.21875 to 0.21875
- norm_moe: float32 [768], replicated, may hold values from 0.1 to 1.9
- router_weight: bfloat16 [768, 16], replicated, may hold values from -0.21875 to 0.21875
- expert_ids: int32 [4, 2048, 1], P('dp', ('seq', 'head')), may hold values from 0 to 15; in each aligned block of 256 rows (0 to 255, 256 to 511, ..., all dimensions but the last counted through in order) at most 32 rows name the same one
- gate_weight: bfloat16 [16, 768, 3072], P(('seq', 'dp'), None, 'head'), may hold values from -0.21875 to 0.21875
- up_weight: bfloat16 [16, 768, 3072], P(('seq', 'dp'), None, 'head'), may hold values from -0.21875 to 0.21875
- down_weight: bfloat16 [16, 3072, 768], P(('seq', 'dp'), 'head'), may hold values from -0.109375 to 0.109375
Outputs:
- layer_out: bfloat16 [4, 2048, 768], P('dp', ('seq', 'head'))
Inputs may be any that keep to these rules, and one draw needn't show every extreme that they name: `expert_ids`: among the rows of one device (aligned blocks of 256 positions, counted over series and positions in order) at most 32 name the same expert, and in every draw some expert is named by exactly 32 rows of some device.
All inputs are finite; a program needn't handle non-finite values.
Results may differ from a plain program's by a relative error of at most 0.0041.
Values may be sent and summed in bfloat16 or wider, within the bound.
A program may use at most 128 MiB of HBM per device.

v0:
```python
import jax
import jax.numpy as jnp
from jax import lax
from jax.sharding import PartitionSpec as P

HD = 128
BLOCK = 512


NORM_EPS = 1e-06


def entering(value, axis, join, neutral):
    count, mine = (lax.axis_size(axis), lax.axis_index(axis))
    pieces = lax.all_gather(value, axis)
    so_far = jnp.full_like(value, 0) + jnp.asarray(neutral, value.dtype)

    def turn(position, so_far):
        longer = join(so_far, pieces[position])
        return jnp.where(position < mine, longer, so_far)

    return lax.fori_loop(0, count - 1, turn, so_far)


def rms_scale(values, gain):
    values = values.astype(jnp.float32)
    return values * lax.rsqrt(jnp.mean(values * values, axis=-1, keepdims=True) + NORM_EPS) * gain


def add_states(earlier_sum, later_sum):
    return earlier_sum + later_sum


def on_device(
    series,
    norm_attn,
    qkv_weight,
    out_weight,
    norm_moe,
    router_weight,
    expert_ids,
    gate_weight,
    up_weight,
    down_weight,
):
    gate_full, up_full = (
        lax.all_gather(gate_weight, "head", axis=2, tiled=True),
        lax.all_gather(up_weight, "head", axis=2, tiled=True),
    )
    down_full = lax.all_gather(down_weight, "head", axis=1, tiled=True)
    tokens_here = series.shape[1]
    model_width = series.shape[2]
    local_heads = qkv_weight.shape[2] // HD
    block_count = tokens_here // BLOCK
    normed_in = rms_scale(series[0], norm_attn).astype(jnp.bfloat16)
    projected = jnp.dot(
        normed_in,
        qkv_weight.reshape(model_width, 3 * local_heads * HD),
        preferred_element_type=jnp.float32,
    ).astype(jnp.bfloat16)
    projected = projected.reshape(block_count, BLOCK, 3, local_heads, HD)
    queries = projected[:, :, 0]
    key_rows = projected[:, :, 1]
    value_rows = projected[:, :, 2]
    block_states = jnp.einsum(
        "bkhd,bkhe->bhde", key_rows, value_rows, preferred_element_type=jnp.float32
    )
    own_state = jnp.sum(block_states, axis=0)
    before = entering(own_state, "seq", add_states, jnp.zeros_like(own_state))
    earlier_blocks = jnp.concatenate(
        [jnp.zeros_like(block_states), jnp.cumsum(block_states, axis=0)[:-1]], axis=0
    )
    states = before[None] + earlier_blocks
    causal = jnp.arange(BLOCK)[:, None] >= jnp.arange(BLOCK)[None, :]
    scores = jnp.einsum("bqhd,bkhd->bhqk", queries, key_rows, preferred_element_type=jnp.float32)
    scores = jnp.where(causal, scores, 0.0).astype(jnp.bfloat16)
    inside = jnp.einsum("bhqk,bkhd->bqhd", scores, value_rows, preferred_element_type=jnp.float32)
    carried = jnp.einsum(
        "bqhd,bhde->bqhe", queries.astype(jnp.float32), states, precision=lax.Precision.HIGHEST
    )
    offset = lax.axis_index("seq") * tokens_here
    position = (offset + jnp.arange(tokens_here, dtype=jnp.int32) + 1).astype(jnp.float32)
    position_scale = (position * jnp.sqrt(jnp.float32(HD))).reshape(block_count, BLOCK, 1, 1)
    mixed_heads = (
        ((inside + carried) / position_scale)
        .astype(jnp.bfloat16)
        .reshape(tokens_here, local_heads * HD)
    )
    own_rows = tokens_here // lax.axis_size("head")
    head_rank = lax.axis_index("head")
    attention = lax.psum_scatter(
        jnp.dot(mixed_heads, out_weight, preferred_element_type=jnp.float32),
        "head",
        scatter_dimension=0,
        tiled=True,
    )
    own_series = lax.dynamic_slice_in_dim(series[0], head_rank * own_rows, own_rows, 0).astype(
        jnp.float32
    )
    residual = own_series + attention
    normed_moe = rms_scale(residual, norm_moe).astype(jnp.bfloat16)
    route_ids = expert_ids[0, :, 0]
    expert_count = router_weight.shape[1]
    capacity = 2 * own_rows // expert_count
    logits = jnp.dot(normed_moe, router_weight, preferred_element_type=jnp.float32)
    picked_expert = route_ids[:, None] == jnp.arange(expert_count, dtype=jnp.int32)[None, :]
    gate_value = jax.nn.sigmoid(
        jnp.sum(jnp.where(picked_expert, logits, 0.0), axis=1, keepdims=True)
    )
    earlier = jnp.arange(own_rows)[None, :] < jnp.arange(own_rows)[:, None]
    same_expert = route_ids[:, None] == route_ids[None, :]
    slot_rank = jnp.sum(jnp.logical_and(same_expert, earlier), axis=1)
    slot_index = route_ids * capacity + slot_rank
    routing = (
        slot_index[:, None] == jnp.arange(expert_count * capacity, dtype=jnp.int32)[None, :]
    ).astype(jnp.bfloat16)
    send_buffer = lax.dot_general(
        routing, normed_moe, (((0,), (0,)), ((), ())), preferred_element_type=jnp.float32
    )
    send_buffer = send_buffer.astype(jnp.bfloat16).reshape(expert_count, capacity, model_width)
    received = lax.all_to_all(send_buffer, ("seq", "dp"), split_axis=0, concat_axis=0, tiled=True)
    flat_rows = received.reshape(-1, model_width)
    gate_proj = jnp.dot(flat_rows, gate_full[0], preferred_element_type=jnp.float32)
    up_proj = jnp.dot(flat_rows, up_full[0], preferred_element_type=jnp.float32)
    hidden = (jax.nn.silu(gate_proj) * up_proj).astype(jnp.bfloat16)
    expert_out = jnp.dot(hidden, down_full[0], preferred_element_type=jnp.float32)
    returned = lax.all_to_all(
        expert_out.astype(jnp.bfloat16).reshape(received.shape),
        ("seq", "dp"),
        split_axis=0,
        concat_axis=0,
        tiled=True,
    )
    routed = jnp.dot(
        routing,
        returned.reshape(expert_count * capacity, model_width),
        preferred_element_type=jnp.float32,
    )
    layer_out = (residual + gate_value * routed).astype(jnp.bfloat16)
    return layer_out[None]


def solution(mesh):
    in_specs = (
        P("dp", "seq", None),
        P(),
        P(None, None, "head"),
        P("head", None),
        P(),
        P(),
        P("dp", ("seq", "head"), None),
        P(("seq", "dp"), None, "head"),
        P(("seq", "dp"), None, "head"),
        P(("seq", "dp"), "head", None),
    )
    out_specs = P("dp", ("seq", "head"), None)
    return jax.shard_map(
        on_device, mesh=mesh, in_specs=in_specs, out_specs=out_specs, check_vma=False
    )
```

profile of v0, /device:TPU:0, one launch (start us, length us, event | category | flops | bytes accessed | tf_op | source)
XLA Modules:
  0.0 143.7 jit_solution(941465656671481594)
XLA Ops:
  6.6 0.8 iota_compare_fusion
  7.4 2.6 %copy.28 = bf16[768,3,384]{0,2,1:T(8,128)(2,1)S(1)} copy(bf16[768,3,384]{2,0,1:T(8,128)(2,1)} %param.14) | data formatting | bytes 3538944 | tf_op args[2]
  10.0 0.2 fusion.5
  10.2 2.3 %convolution_convert_fusion = bf16[512,1152]{1,0:T(8,128)(2,1)} fusion(bf16[768,1152]{0,1:T(8,128)(2,1)S(1)} %bitcast.83, bf16[1,512,768]{2,1,0:T(8,128)(2,1)S(1)} %copy-done.2, f32[768]{0:T(1024)S(1)} %copy-done.6, f32[512]{0:T(512)S(1)} %add_rsqrt_fusion), kind=kOutput, calls=%fused_computation.8 | convolution fusion | flops 908132352 | bytes 3740672 | tf_op jit(solution)/shard_map/dot_general | solution.py:56
  12.5 1.6 %copy.29 = bf16[512,1152]{0,1:T(8,128)(2,1)S(1)} copy(bf16[512,1152]{1,0:T(8,128)(2,1)} %convolution_convert_fusion) | data formatting | bytes 2359296 | tf_op jit(solution)/shard_map/convert_element_type | solution.py:60
  14.1 0.3 fusion.24
  14.4 21.3 %all-gather = f32[12,128,128]{2,1,0:T(8,128)S(1)} all-gather(f32[3,128,128]{2,1,0:T(8,128)S(1)} %fusion.24), channel_id=2, replica_groups=mesh['seq'=4,'head'=2,'dp'=4] {'seq'}, dimensions={0}, use_global_device_ids=true | all-gather | bytes 983040 | tf_op jit(solution)/shard_map/all_gather | solution.py:15
  35.6 0.2 while.14
  35.6 0.1 add_select_fusion.2
  35.7 0.1 add_select_fusion.2
  35.8 0.1 add_select_fusion.2
  35.9 0.5 fusion.25
  36.4 2.8 %fusion.19 = bf16[1,3,128,512]{3,2,1,0:T(8,128)(2,1)} fusion(f32[3,128,512]{2,1,0:T(8,128)S(1)} %fusion.25, pred[512,512]{1,0:T(8,128)(4,1)} %iota_compare_fusion, f32[512]{0:T(512)S(1)} %convert_multiply_fusion.2, bf16[1,512,3,3,128]{1,4,3,2,0:T(8,128)(2,1)S(1)} %bitcast.82), kind=kOutput, calls=%fused_computation.27 | convolution fusion | flops 404815872 | bytes 2623488 | tf_op jit(solution)/shard_map/bhqk,bkhd->bqhd/dot_general | solution.py:77
  39.2 2.7 %fusion.30 = f32[512,768]{1,0:T(8,128)} fusion(bf16[512,384]{0,1:T(8,128)(2,1)} %bitcast.85, bf16[384,768]{1,0:T(8,128)(2,1)S(1)} %copy-done), kind=kOutput, calls=%fused_computation.52 | convolution fusion | flops 301989888 | bytes 2555904 | tf_op jit(solution)/shard_map/dot_general | solution.py:92
  42.0 0.0 all-gather.5.cloned.1.call-start
  42.0 0.7 all-gather.5.cloned.1.call-update
  42.8 0.7 all-gather.7.cloned.1.call-update
  43.5 0.5 all-gather.9.cloned.1.call-update
  44.1 0.2 convert_reduce_fusion
  44.3 6.3 %reduce-scatter.2.cloned.1.call-done = f32[256,768]{1,0:T(8,128)} async-done(((f32[512,768]{1,0:T(8,128)}), f32[256,768]{1,0:T(8,128)}) %reduce-scatter.2.cloned.1.call-update) | async-done | bytes 786448 | tf_op jit(solution)/shard_map/reduce_scatter | solution.py:91
  50.5 1.3 multiply_reduce_fusion
  51.9 1.3 multiply_convert_fusion.1
  53.2 0.6 convolution_convert_fusion.1
  53.7 28.3 %all_to_all.10 = bf16[16,32,768]{2,1,0:T(8,128)(2,1)S(1)} all-to-all(bf16[16,32,768]{2,1,0:T(8,128)(2,1)S(1)} %bitcast.79), channel_id=1, replica_groups=mesh['seq'=4,'head'=2,'dp'=4] {'seq','dp'}, dimensions={0} | all-to-all | bytes 1572864 | tf_op jit(solution)/shard_map/all_to_all | solution.py:121
  82.1 6.8 %fusion.3 = f32[512,3072]{1,0:T(8,128)} fusion(bf16[512,768]{1,0:T(8,128)(2,1)S(1)} %bitcast.76, bf16[1,768,3072]{2,1,0:T(8,128)(2,1)} %all-gather.5.cloned.1.call-done), kind=kOutput, calls=%fused_computation.5 | convolution fusion | flops 2415919104 | bytes 11796480 | tf_op jit(solution)/shard_map/dot_general | solution.py:123
  88.9 7.9 %multiply_convert_fusion = bf16[512,3072]{1,0:T(8,128)(2,1)} fusion(f32[512,3072]{1,0:T(8,128)} %fusion.3, bf16[512,768]{1,0:T(8,128)(2,1)S(1)} %bitcast.77, bf16[1,768,3072]{2,1,0:T(8,128)(2,1)} %all-gather.7.cloned.1.call-done), kind=kOutput, calls=%fused_computation.1 | convolution fusion | flops 2425356288 | bytes 14942208 | tf_op jit(solution)/shard_map/dot_general | solution.py:124
  96.7 5.5 %all-gather.9.cloned.1.call-done = bf16[1,3072,768]{2,1,0:T(8,128)(2,1)} async-done(((bf16[1,1536,768]{2,1,0:T(8,128)(2,1)}), bf16[1,3072,768]{2,1,0:T(8,128)(2,1)}) %all-gather.9.cloned.1.call-update) | async-done | bytes 4718608 | tf_op jit(solution)/shard_map/all_gather | solution.py:50
  102.2 6.8 %fusion.9 = bf16[512,768]{1,0:T(8,128)(2,1)} fusion(bf16[512,3072]{1,0:T(8,128)(2,1)} %multiply_convert_fusion, bf16[1,3072,768]{2,1,0:T(8,128)(2,1)} %all-gather.9.cloned.1.call-done), kind=kOutput, calls=%fused_computation.15 | convolution fusion | flops 2416312320 | bytes 8650752 | tf_op jit(solution)/shard_map/dot_general | solution.py:126
  109.0 6.9 %all-to-all-start.1 = ((bf16[16,32,768]{2,1,0:T(8,128)(2,1)}), bf16[16,32,768]{2,1,0:T(8,128)(2,1)S(1)}, u32[]{:S(2)}, u32[]{:S(2)}) async-start(bf16[16,32,768]{2,1,0:T(8,128)(2,1)} %bitcast.84), calls=%async_computation.2 | async-start | bytes 1572864 | tf_op jit(solution)/shard_map/all_to_all | solution.py:127
  115.9 0.3 fusion.17
  116.2 19.8 %all-to-all-done.1 = bf16[16,32,768]{2,1,0:T(8,128)(2,1)S(1)} async-done(((bf16[16,32,768]{2,1,0:T(8,128)(2,1)}), bf16[16,32,768]{2,1,0:T(8,128)(2,1)S(1)}, u32[]{:S(2)}, u32[]{:S(2)}) %all-to-all-start.1) | async-done | bytes 786464 | tf_op jit(solution)/shard_map/all_to_all | solution.py:127
  136.0 1.2 fusion.16
  (26 shorter events, 0.2 us)
Async XLA Ops:
  6.5 32.7 %copy-start = (bf16[384,768]{1,0:T(8,128)(2,1)S(1)}, bf16[384,768]{1,0:T(8,128)(2,1)}, u32[]{:S(2)}) copy-start(bf16[384,768]{1,0:T(8,128)(2,1)} %param.15) | copy-start | bytes 1769476
  6.5 3.4 %copy-start.2 = (bf16[1,512,768]{2,1,0:T(8,128)(2,1)S(1)}, bf16[1,512,768]{2,1,0:T(8,128)(2,1)}, u32[]{:S(2)}) copy-start(bf16[1,512,768]{2,1,0:T(8,128)(2,1)} %param.12) | copy-start | bytes 2359300
  6.5 3.7 %copy-start.6 = (f32[768]{0:T(1024)S(1)}, f32[768]{0:T(1024)}, u32[]{:S(2)}) copy-start(f32[768]{0:T(1024)} %param.13) | copy-start | bytes 9220
  6.5 44.0 %reduce-scatter.2.cloned.1.call-start = ((), (), s32[]{:S(2)}) async-start(), calls=%async_computation.3 | async-start | bytes 2359296 | tf_op jit(solution)/shard_map/reduce_scatter | solution.py:91
  42.0 40.1 %all-gather.5.cloned.1.call-start = ((), (), s32[]{:S(2)}) async-start(), calls=%async_computation.4 | async-start | bytes 7077888 | tf_op jit(solution)/shard_map/all_gather | solution.py:47
  42.7 1.3 copy-start.4
  42.7 46.1 %all-gather.7.cloned.1.call-start = ((), (), s32[]{:S(2)}) async-start(), calls=%async_computation.5 | async-start | bytes 7077888 | tf_op jit(solution)/shard_map/all_gather | solution.py:48
  43.5 8.4 %copy-start.5 = (f32[768]{0:T(1024)S(1)}, f32[768]{0:T(1024)}, u32[]{:S(2)}) copy-start(f32[768]{0:T(1024)} %param.16) | copy-start | bytes 9220
  43.5 58.7 %all-gather.9.cloned.1.call-start = ((), (), s32[]{:S(2)}) async-start(), calls=%async_computation.6 | async-start | bytes 7077888 | tf_op jit(solution)/shard_map/all_gather | solution.py:50
  96.7 19.2 %copy-start.3 = (bf16[768,16]{0,1:T(8,128)(2,1)S(1)}, bf16[768,16]{0,1:T(8,128)(2,1)}, u32[]{:S(2)}) copy-start(bf16[768,16]{0,1:T(8,128)(2,1)} %param.17) | copy-start | bytes 73732
  109.0 27.0 %copy-start.1 = (f32[256,768]{1,0:T(8,128)S(1)}, f32[256,768]{1,0:T(8,128)}, u32[]{:S(2)}) copy-start(f32[256,768]{1,0:T(8,128)} %reduce-scatter.2.cloned.1.call-done) | copy-start | bytes 2359300
  109.0 27.0 %all-to-all-start.1 = ((bf16[16,32,768]{2,1,0:T(8,128)(2,1)}), bf16[16,32,768]{2,1,0:T(8,128)(2,1)S(1)}, u32[]{:S(2)}, u32[]{:S(2)}) async-start(bf16[16,32,768]{2,1,0:T(8,128)(2,1)} %bitcast.84), calls=%async_computation.2 | async-start | bytes 1572864 | tf_op jit(solution)/shard_map/all_to_all | solution.py:127
Sparse Core Ops, SparseCore 0:
  42.1 8.4 reduce-scatter.1
  52.2 15.6 all-gather.4
  69.5 15.6 all-gather.6
  86.6 15.6 all-gather.8
where the time goes:
time: 144 us
  blocking collectives  49.6 us (34%)
  waiting for transfers between devices  33.5 us (23%)
  matrix products  32 us (22%)
  between operations  13.3 us (9%)
  starting transfers between devices  7.03 us (5%)
  local copies, waits for them, and re-layouts  4.22 us (3%)
  other arithmetic  4 us (3%)
    all_to_all x1, blocking collectives, on_device(): lax.all_to_all(send_buffer, ('seq', 'dp'), split_axis=0, concat_axis=0, t...  28.3 us
    all_gather x1, blocking collectives, entering(): pieces = lax.all_gather(value, axis)  21.3 us
    all_to_all x1, waiting for transfers between devices, on_device(): lax.all_to_all(expert_out.astype(jnp.bfloat16).reshape(received.shape), (...  19.8 us
    dot_general x1, matrix products, on_device(): up_proj = jnp.dot(flat_rows, up_full[0], preferred_element_type=jnp.float32)  7.85 us
    all_to_all x1, starting transfers between devices, on_device(): lax.all_to_all(expert_out.astype(jnp.bfloat16).reshape(received.shape), (...  6.91 us
    dot_general x1, matrix products, on_device(): jnp.dot(flat_rows, gate_full[0], preferred_element_type=jnp.float32)  6.8 us
    dot_general x1, matrix products, on_device(): jnp.dot(hidden, down_full[0], preferred_element_type=jnp.float32)  6.77 us
    reduce_scatter x1, waiting for transfers between devices, on_device(): lax.psum_scatter(jnp.dot(mixed_heads, out_weight, preferred_element_type=...  6.28 us
  transfers between devices with their start and end apart: 5, of which 3 were waited for; matrix products, arithmetic and copies ran while one was open for 13% of the time, Pallas kernels for 0%

commit v1 on v0

v1 whole, which is shorter than its diff:
```python
import functools

import jax
import jax.numpy as jnp
from jax import lax
from jax.experimental import pallas as pl
from jax.experimental.pallas import tpu as pltpu
from jax.sharding import PartitionSpec as P

HD = 128
BLOCK = 512
NORM_EPS = 1e-06
MESH = pl.DeviceIdType.MESH
F32 = jnp.float32
BF16 = jnp.bfloat16


def rms_scale(values, gain):
    return values * lax.rsqrt(jnp.mean(values * values, axis=-1, keepdims=True) + NORM_EPS) * gain


def dot(a, b, dims=((1,), (0,))):
    return lax.dot_general(a, b, (dims, ((), ())), preferred_element_type=F32)


def layer_kernel(
    seq_n,
    dp_n,
    cap,
    series,
    norm_attn,
    qkv_weight,
    out_weight,
    norm_moe,
    router_weight,
    expert_ids,
    gate_hbm,
    up_hbm,
    down_hbm,
    layer_out,
    gate_v,
    up_v,
    down_v,
    normed,
    projected,
    state_own,
    state_in,
    before,
    inside,
    partial_out,
    partial_in,
    residual,
    routing,
    send_rows,
    recv_rows,
    out_rows,
    back_rows,
    own_sem,
    w_send,
    w_recv,
    s_send,
    s_recv,
    r_send,
    r_recv,
    d_send,
    d_recv,
    b_send,
    b_recv,
):
    z = lax.axis_index("seq")
    head = lax.axis_index("head")
    y = lax.axis_index("dp")
    other = 1 - head
    me = z * dp_n + y
    tokens, width = series.shape
    rows = tokens // 2
    local = qkv_weight.shape[1] // 3
    heads = local // HD
    half = rows

    def step_of(i):
        return (1 + (seq_n // 2 + i - 2 + seq_n - 1) % (seq_n - 1)) * ((i + seq_n - 1) // seq_n)

    def for_peers(i, sign, act):
        k = step_of(i)
        there = (z + sign * k + seq_n) % seq_n
        for d in range(dp_n):
            col = (y + sign * d + dp_n) % dp_n
            if d == 0:
                @pl.when(k != 0)
                def _():
                    act(there, col)
            else:
                act(there, col)
        return there

    def slab(expert):
        return pl.ds(pl.multiple_of(expert * cap, cap), cap)

    barrier = pltpu.get_barrier_semaphore()
    pl.semaphore_signal(barrier, inc=1, device_id={"head": other}, device_id_type=MESH)

    def greet(i, carry):
        for_peers(
            i,
            1,
            lambda a, b: pl.semaphore_signal(
                barrier, inc=1, device_id={"seq": a, "dp": b}, device_id_type=MESH
            ),
        )
        return carry

    lax.fori_loop(0, seq_n, greet, 0)

    weights = ((gate_hbm, gate_v), (up_hbm, up_v), (down_hbm, down_v))
    own_copies = [
        pltpu.make_async_copy(src.at[0], dst.at[0], own_sem.at[j])
        for j, (src, dst) in enumerate(weights)
    ]
    far_copies = [
        pltpu.make_async_remote_copy(
            src_ref=src.at[0],
            dst_ref=dst.at[1],
            send_sem=w_send.at[j],
            recv_sem=w_recv.at[j],
            device_id={"head": other},
            device_id_type=MESH,
        )
        for j, (src, dst) in enumerate(weights)
    ]
    for copy in own_copies:
        copy.start()

    normed[...] = rms_scale(series[...].astype(F32), norm_attn[...]).astype(BF16)
    projected[:, local:] = dot(normed[...], qkv_weight[:, local:]).astype(BF16)
    for h in range(heads):
        at = pl.ds(h * HD, HD)
        keys = projected[:, local + h * HD : local + (h + 1) * HD]
        values = projected[:, 2 * local + h * HD : 2 * local + (h + 1) * HD]
        state_own[at, :] = dot(keys, values, ((0,), (0,))).astype(BF16)

    pl.semaphore_wait(barrier, seq_n * dp_n)

    def state_copy(to):
        return pltpu.make_async_remote_copy(
            src_ref=state_own,
            dst_ref=state_in.at[z],
            send_sem=s_send.at[to],
            recv_sem=s_recv.at[z],
            device_id={"seq": to},
            device_id_type=MESH,
        )

    def send_state(j, carry):
        state_copy(seq_n - 1 - j).start()
        return carry

    lax.fori_loop(0, seq_n - 1 - z, send_state, 0)
    far_copies[0].start()
    far_copies[1].start()

    projected[:, :local] = dot(normed[...], qkv_weight[:, :local]).astype(BF16)
    for h in range(heads):
        cols = slice(h * HD, (h + 1) * HD)
        for part in range(2):
            low, high = part * half, (part + 1) * half
            q = projected[low:high, cols]
            keys = projected[:high, local + h * HD : local + (h + 1) * HD]
            values = projected[:high, 2 * local + h * HD : 2 * local + (h + 1) * HD]
            scores = dot(q, keys, ((1,), (1,)))
            t = lax.broadcasted_iota(jnp.int32, scores.shape, 0) + low
            s = lax.broadcasted_iota(jnp.int32, scores.shape, 1)
            scores = jnp.where(t >= s, scores, 0.0).astype(BF16)
            inside[low:high, cols] = dot(scores, values)

    ids = expert_ids[...]
    experts = router_weight.shape[1]
    picked = ids == lax.broadcasted_iota(jnp.int32, (rows, experts), 1)
    picked_f = picked.astype(F32)
    earlier = lax.broadcasted_iota(jnp.int32, (rows, rows), 1) < lax.broadcasted_iota(
        jnp.int32, (rows, rows), 0
    )
    ranks = dot(earlier.astype(F32).astype(BF16), picked_f.astype(BF16))
    rank = jnp.sum(ranks * picked_f, axis=1, keepdims=True)
    slot = ids * cap + rank.astype(jnp.int32)
    routing[...] = (
        (slot == lax.broadcasted_iota(jnp.int32, routing.shape, 1)).astype(F32).astype(BF16)
    )

    before[...] = jnp.zeros_like(before)

    def add_state(j, carry):
        pltpu.make_async_remote_copy(
            src_ref=state_own,
            dst_ref=state_in.at[j],
            send_sem=s_send.at[j],
            recv_sem=s_recv.at[j],
            device_id={"seq": j},
            device_id_type=MESH,
        ).wait_recv()
        before[...] += state_in[j].astype(F32)
        return carry

    lax.fori_loop(0, z, add_state, 0)

    state_hi = before[...].astype(BF16)
    state_lo = (before[...] - state_hi.astype(F32)).astype(BF16)

    def project_out(which):
        start = pl.multiple_of(which * half, half)
        at = pl.ds(start, half)
        position = z * tokens + start + 1 + lax.broadcasted_iota(jnp.int32, (half, 1), 0)
        scale = 1.0 / (position.astype(F32) * jnp.sqrt(F32(HD)))
        mixed = []
        for h in range(heads):
            cols = slice(h * HD, (h + 1) * HD)
            q = projected[at, cols]
            carried = dot(q, state_hi[cols]) + dot(q, state_lo[cols])
            mixed.append(((inside[at, cols] + carried) * scale).astype(BF16))
        return dot(jnp.concatenate(mixed, axis=1), out_weight[...])

    partial_out[...] = project_out(other)
    sum_copy = pltpu.make_async_remote_copy(
        src_ref=partial_out,
        dst_ref=partial_in,
        send_sem=r_send,
        recv_sem=r_recv,
        device_id={"head": other},
        device_id_type=MESH,
    )
    sum_copy.start()
    far_copies[2].start()
    own_at = pl.ds(pl.multiple_of(head * half, half), half)
    residual[...] = project_out(head) + series[own_at, :].astype(F32)
    sum_copy.wait_recv()
    total = residual[...] + partial_in[...]
    residual[...] = total
    normed_moe = rms_scale(total, norm_moe[...]).astype(BF16)
    send_rows[...] = dot(routing[...], normed_moe, ((0,), (0,))).astype(BF16)

    def row_copy(to_z, to_y):
        to = to_z * dp_n + to_y
        return pltpu.make_async_remote_copy(
            src_ref=send_rows.at[slab(to)],
            dst_ref=recv_rows.at[slab(me)],
            send_sem=d_send.at[to],
            recv_sem=d_recv.at[me],
            device_id={"seq": to_z, "dp": to_y},
            device_id_type=MESH,
        )

    def row_arrival(from_z, from_y):
        source = from_z * dp_n + from_y
        return pltpu.make_async_remote_copy(
            src_ref=send_rows.at[slab(source)],
            dst_ref=recv_rows.at[slab(source)],
            send_sem=d_send.at[source],
            recv_sem=d_recv.at[source],
            device_id={"seq": from_z, "dp": from_y},
            device_id_type=MESH,
        )

    def back_copy(to_z, to_y):
        to = to_z * dp_n + to_y
        return pltpu.make_async_remote_copy(
            src_ref=out_rows.at[slab(to)],
            dst_ref=back_rows.at[slab(me)],
            send_sem=b_send.at[to],
            recv_sem=b_recv.at[me],
            device_id={"seq": to_z, "dp": to_y},
            device_id_type=MESH,
        )

    def back_arrival(from_z, from_y):
        source = from_z * dp_n + from_y
        return pltpu.make_async_remote_copy(
            src_ref=out_rows.at[slab(source)],
            dst_ref=back_rows.at[slab(source)],
            send_sem=b_send.at[source],
            recv_sem=b_recv.at[source],
            device_id={"seq": from_z, "dp": from_y},
            device_id_type=MESH,
        )

    def dispatch(i, carry):
        for_peers(i, 1, lambda a, b: row_copy(a, b).start())
        return carry

    lax.fori_loop(0, seq_n, dispatch, 0)
    recv_rows[slab(me), :] = send_rows[slab(me), :]

    logits = dot(normed_moe, router_weight[...])
    gate_value = jax.nn.sigmoid(jnp.sum(logits * picked_f, axis=1, keepdims=True))

    for copy in own_copies:
        copy.wait()
    for copy in far_copies:
        copy.wait()

    group = dp_n * cap
    units = gate_v.shape[2]
    tile = units // 3

    def expert_group(i, carry):
        source_z = for_peers(i, -1, lambda a, b: row_arrival(a, b).wait_recv())
        at = pl.ds(pl.multiple_of(source_z * group, group), group)
        x = recv_rows[at, :]
        acc = jnp.zeros((group, width), F32)
        for side in range(2):
            for c in range(units // tile):
                cols = slice(c * tile, (c + 1) * tile)
                g = dot(x, gate_v[side, :, cols])
                u = dot(x, up_v[side, :, cols])
                hidden = (g * jax.nn.sigmoid(g) * u).astype(BF16)
                acc = acc + dot(hidden, down_v[side, cols, :])
        out_rows[at, :] = acc.astype(BF16)
        for_peers(i, -1, lambda a, b: back_copy(a, b).start())
        return carry

    lax.fori_loop(0, seq_n, expert_group, 0)
    back_rows[slab(me), :] = out_rows[slab(me), :]

    def await_back(i, carry):
        for_peers(i, 1, lambda a, b: back_arrival(a, b).wait_recv())
        return carry

    lax.fori_loop(0, seq_n, await_back, 0)
    routed = dot(routing[...], back_rows[...])
    layer_out[...] = (residual[...] + gate_value * routed).astype(BF16)

    def sent_rows(i, carry):
        for_peers(i, 1, lambda a, b: row_copy(a, b).wait_send())
        for_peers(i, -1, lambda a, b: back_copy(a, b).wait_send())
        return carry

    lax.fori_loop(0, seq_n, sent_rows, 0)

    def sent_state(j, carry):
        state_copy(seq_n - 1 - j).wait_send()
        return carry

    lax.fori_loop(0, seq_n - 1 - z, sent_state, 0)
    sum_copy.wait_send()


def on_device(
    series,
    norm_attn,
    qkv_weight,
    out_weight,
    norm_moe,
    router_weight,
    expert_ids,
    gate_weight,
    up_weight,
    down_weight,
):
    seq_n, head_n, dp_n = lax.axis_size("seq"), lax.axis_size("head"), lax.axis_size("dp")
    tokens, width = series.shape[1:]
    assert head_n == 2 and tokens == BLOCK and seq_n > 1
    rows = tokens // 2
    experts = router_weight.shape[1]
    peers = seq_n * dp_n
    assert experts == peers
    local = qkv_weight.shape[2]
    units = gate_weight.shape[2]
    capacity = 2 * rows // experts
    cap = -(-capacity // 16) * 16
    slots = experts * cap
    vmem = pl.BlockSpec(memory_space=pltpu.VMEM)
    hbm = pl.BlockSpec(memory_space=pl.ANY)
    dma = pltpu.SemaphoreType.DMA
    out = pl.pallas_call(
        functools.partial(layer_kernel, seq_n, dp_n, cap),
        out_shape=jax.ShapeDtypeStruct((rows, width), BF16),
        in_specs=[vmem] * 7 + [hbm] * 3,
        out_specs=vmem,
        scratch_shapes=[
            pltpu.VMEM((2, width, units), BF16),
            pltpu.VMEM((2, width, units), BF16),
            pltpu.VMEM((2, units, width), BF16),
            pltpu.VMEM((tokens, width), BF16),
            pltpu.VMEM((tokens, 3 * local), BF16),
            pltpu.VMEM((local, HD), BF16),
            pltpu.VMEM((seq_n, local, HD), BF16),
            pltpu.VMEM((local, HD), F32),
            pltpu.VMEM((tokens, local), F32),
            pltpu.VMEM((rows, width), F32),
            pltpu.VMEM((rows, width), F32),
            pltpu.VMEM((rows, width), F32),
            pltpu.VMEM((rows, slots), BF16),
            pltpu.VMEM((slots, width), BF16),
            pltpu.VMEM((slots, width), BF16),
            pltpu.VMEM((slots, width), BF16),
            pltpu.VMEM((slots, width), BF16),
            dma((3,)),
            dma((3,)),
            dma((3,)),
            dma((seq_n,)),
            dma((seq_n,)),
            dma,
            dma,
            dma((peers,)),
            dma((peers,)),
            dma((peers,)),
            dma((peers,)),
        ],
        compiler_params=pltpu.CompilerParams(
            collective_id=0, has_side_effects=True, vmem_limit_bytes=56 * 1024 * 1024
        ),
        name="layer",
    )(
        series[0],
        norm_attn[None],
        qkv_weight.reshape(width, 3 * local),
        out_weight,
        norm_moe[None],
        router_weight,
        expert_ids[0],
        gate_weight,
        up_weight,
        down_weight,
    )
    return out[None]


def solution(mesh):
    in_specs = (
        P("dp", "seq", None),
        P(),
        P(None, None, "head"),
        P("head", None),
        P(),
        P(),
        P("dp", ("seq", "head"), None),
        P(("seq", "dp"), None, "head"),
        P(("seq", "dp"), None, "head"),
        P(("seq", "dp"), "head", None),
    )
    out_specs = P("dp", ("seq", "head"), None)
    return jax.shard_map(
        on_device, mesh=mesh, in_specs=in_specs, out_specs=out_specs, check_vma=False
    )
```

time: 144 us -> 73.2 us (0.51)
  Pallas kernels: 0 us -> 63.4 us
  blocking collectives: 49.6 us -> 0 us
  waiting for transfers between devices: 33.5 us -> 0 us
  matrix products: 32 us -> 0 us
  between operations: 13.3 us -> 0.05 us
  starting transfers between devices: 7.03 us -> 0 us
  local copies, waits for them, and re-layouts: 4.22 us -> 9.46 us
  other arithmetic: 4 us -> 0 us
    pallas_call x0 -> x1, Pallas kernels: none -> 63.4 us  [on_device(): pl.pallas_call(functools.partial(layer_kernel, seq_n, dp_n, cap), out_sha...]
    dot_general x11 -> x0, matrix products: 32 us -> none  [the longest x1 7.85 us: on_device(): up_proj = jnp.dot(flat_rows, up_full[0], preferred_element_type=jnp.float32)]
    all_to_all x1 -> x0, blocking collectives: 28.3 us -> none  [on_device(): lax.all_to_all(send_buffer, ('seq', 'dp'), split_axis=0, concat_axis=0, t...]
    all_gather x1 -> x0, blocking collectives: 21.3 us -> none  [entering(): pieces = lax.all_gather(value, axis)]
    all_to_all x1 -> x0, waiting for transfers between devices: 19.8 us -> none  [on_device(): lax.all_to_all(expert_out.astype(jnp.bfloat16).reshape(received.shape), (...]
    all_to_all x1 -> x0, starting transfers between devices: 6.91 us -> none  [on_device(): lax.all_to_all(expert_out.astype(jnp.bfloat16).reshape(received.shape), (...]
    reduce_scatter x1 -> x0, waiting for transfers between devices: 6.28 us -> none  [on_device(): lax.psum_scatter(jnp.dot(mixed_heads, out_weight, preferred_element_type=...]
    all_gather x3 -> x0, waiting for transfers between devices: 5.49 us -> none  [the longest x1 5.49 us: on_device(): down_full = lax.all_gather(down_weight, 'head', axis=1, tiled=True)]
  transfers between devices with their start and end apart: 5 -> 0, of which waited for: 3 -> 0; matrix products, arithmetic and copies ran while one was open for 13% -> 0% of each run, Pallas kernels for 0% -> 0%
where the time goes in v1:
time: 73.2 us; the launch traced here: 72.9 us
  Pallas kernels  63.4 us (87%)
  local copies, waits for them, and re-layouts  9.46 us (13%)
    pallas_call x1, Pallas kernels, on_device(): pl.pallas_call(functools.partial(layer_kernel, seq_n, dp_n, cap), out_sha...  63.4 us
    unnamed x11, local copies, waits for them, and re-layouts  5.23 us
    reshape x1, local copies, waits for them, and re-layouts, on_device(): qkv_weight.reshape(width, 3 * local)  2.25 us

profile of v1, /device:TPU:0, one launch (start us, length us, event | category | flops | bytes accessed | tf_op | source)
XLA Modules:
  0.0 72.9 jit_solution(8739121852823785751)
XLA Ops:
  0.0 2.6 %copy.13 = bf16[768,3,384]{0,2,1:T(8,128)(2,1)S(1)} copy(bf16[768,3,384]{2,0,1:T(8,128)(2,1)} %param.12) | data formatting | bytes 3538944 | tf_op args[2]
  2.6 0.0 copy-start
  2.6 0.0 copy-start.3
  2.7 0.0 copy-start.1
  2.7 0.0 copy-start.2
  2.7 2.3 %copy.14.qkv_weight = bf16[768,1152]{1,0:T(8,128)(2,1)} copy(bf16[768,1152]{0,1:T(8,128)(2,1)S(1)} %bitcast.4) | data formatting | bytes 3538944 | tf_op jit(solution)/shard_map/reshape | solution.py:415
  4.9 0.0 copy-done
  4.9 0.8 %copy.15.router_weight = bf16[768,16]{1,0:T(8,128)(2,1)} copy(bf16[768,16]{0,1:T(8,128)(2,1)S(1)} %copy-done) | data formatting | bytes 49152 | tf_op args[5]
  5.7 0.0 copy-done.3
  5.8 0.8 %copy.16.expert_ids = s32[256,1]{1,0:T(8,128)} copy(s32[256,1]{0,1:T(1,128)S(1)} %bitcast.7) | data formatting | bytes 2048 | tf_op jit(solution)/shard_map/squeeze | solution.py:419
  6.5 0.0 copy-done.1
  6.5 0.6 broadcast_in_dim.10.norm_moe
  7.1 0.0 copy-done.2
  7.1 0.6 broadcast_in_dim.9.norm_attn
  7.7 63.4 %layer.1 = bf16[256,768]{1,0:T(8,128)(2,1)} custom-call(bf16[512,768]{1,0:T(8,128)(2,1)} %bitcast.6, f32[1,768]{1,0:T(1,128)} %broadcast_in_dim.9.norm_attn, bf16[768,1152]{1,0:T(8,128)(2,1)} %copy.14.qkv_weight, bf16[384,768]{1,0:T(8,128)(2,1)} %out_weight.1, f32[1,768]{1,0:T(1,128)} %broadcast_in_dim.10.norm_moe, bf16[768,16]{1,0:T(8,128)(2,1)} %copy.15.router_weight, ...), custom_call_target="tpu_custom_call" | custom-call | tf_op jit(solution)/shard_map/layer/pallas_call | solution.py:373
  71.2 1.8 %copy.18 = bf16[1,256,768]{2,1,0:T(8,128)(2,1)} copy(bf16[1,256,768]{2,1,0:T(8,128)(2,1)} %bitcast.5) | data formatting | bytes 786432
Async XLA Ops:
  2.6 2.3 %copy-start = (bf16[768,16]{0,1:T(8,128)(2,1)S(1)}, bf16[768,16]{0,1:T(8,128)(2,1)}, u32[]{:S(2)}) copy-start(bf16[768,16]{0,1:T(8,128)(2,1)} %param.15) | copy-start | bytes 73732
  2.6 3.1 %copy-start.3 = (s32[1,256,1]{1,2,0:T(1,128)S(1)}, s32[1,256,1]{1,2,0:T(1,128)}, u32[]{:S(2)}) copy-start(s32[1,256,1]{1,2,0:T(1,128)} %param.16) | copy-start | bytes 3076
  2.7 3.9 %copy-start.1 = (f32[768]{0:T(1024)S(1)}, f32[768]{0:T(1024)}, u32[]{:S(2)}) copy-start(f32[768]{0:T(1024)} %param.14) | copy-start | bytes 9220
  2.7 4.5 %copy-start.2 = (f32[768]{0:T(1024)S(1)}, f32[768]{0:T(1024)}, u32[]{:S(2)}) copy-start(f32[768]{0:T(1024)} %param.11) | copy-start | bytes 9220

commit v2 on v1

--- a/solution.py
+++ b/solution.py
@@ -51,6 +51,8 @@
     partial_in,
     residual,
     routing,
+    placing,
+    hidden,
     send_rows,
     recv_rows,
     out_rows,
@@ -74,7 +76,7 @@
     me = z * dp_n + y
     tokens, width = series.shape
     rows = tokens // 2
-    local = qkv_weight.shape[1] // 3
+    local = qkv_weight.shape[2]
     heads = local // HD
     half = rows
 
@@ -131,8 +133,9 @@
     for copy in own_copies:
         copy.start()
 
-    normed[...] = rms_scale(series[...].astype(F32), norm_attn[...]).astype(BF16)
-    projected[:, local:] = dot(normed[...], qkv_weight[:, local:]).astype(BF16)
+    normed[...] = rms_scale(series[...].astype(F32), norm_attn[...][None]).astype(BF16)
+    for j in (1, 2):
+        projected[:, j * local : (j + 1) * local] = dot(normed[...], qkv_weight[j]).astype(BF16)
     for h in range(heads):
         at = pl.ds(h * HD, HD)
         keys = projected[:, local + h * HD : local + (h + 1) * HD]
@@ -159,7 +162,7 @@
     far_copies[0].start()
     far_copies[1].start()
 
-    projected[:, :local] = dot(normed[...], qkv_weight[:, :local]).astype(BF16)
+    projected[:, :local] = dot(normed[...], qkv_weight[0]).astype(BF16)
     for h in range(heads):
         cols = slice(h * HD, (h + 1) * HD)
         for part in range(2):
@@ -174,18 +177,26 @@
             inside[low:high, cols] = dot(scores, values)
 
     ids = expert_ids[...]
-    experts = router_weight.shape[1]
-    picked = ids == lax.broadcasted_iota(jnp.int32, (rows, experts), 1)
-    picked_f = picked.astype(F32)
-    earlier = lax.broadcasted_iota(jnp.int32, (rows, rows), 1) < lax.broadcasted_iota(
-        jnp.int32, (rows, rows), 0
-    )
-    ranks = dot(earlier.astype(F32).astype(BF16), picked_f.astype(BF16))
-    rank = jnp.sum(ranks * picked_f, axis=1, keepdims=True)
+    experts = router_weight.shape[0]
+    slots = routing.shape[1]
+    picked_row = (ids == lax.broadcasted_iota(jnp.int32, (experts, rows), 0)).astype(F32)
+    earlier = lax.broadcasted_iota(jnp.int32, (rows, rows), 0) < lax.broadcasted_iota(
+        jnp.int32, (rows, rows), 1
+    )
+    ranks = dot(picked_row.astype(BF16), earlier.astype(F32).astype(BF16))
+    rank = jnp.sum(ranks * picked_row, axis=0, keepdims=True)
     slot = ids * cap + rank.astype(jnp.int32)
+    placing[...] = (
+        (slot == lax.broadcasted_iota(jnp.int32, (slots, rows), 0)).astype(F32).astype(BF16)
+    )
+    columns = jnp.transpose(jnp.broadcast_to(slot.astype(F32), (HD, rows)))
+    slot_column = columns[:, :1].astype(jnp.int32)
     routing[...] = (
-        (slot == lax.broadcasted_iota(jnp.int32, routing.shape, 1)).astype(F32).astype(BF16)
-    )
+        (slot_column == lax.broadcasted_iota(jnp.int32, (rows, slots), 1)).astype(F32).astype(BF16)
+    )
+    picked = (
+        slot_column // cap == lax.broadcasted_iota(jnp.int32, (rows, experts), 1)
+    ).astype(F32)
 
     before[...] = jnp.zeros_like(before)
 
@@ -235,8 +246,8 @@
     sum_copy.wait_recv()
     total = residual[...] + partial_in[...]
     residual[...] = total
-    normed_moe = rms_scale(total, norm_moe[...]).astype(BF16)
-    send_rows[...] = dot(routing[...], normed_moe, ((0,), (0,))).astype(BF16)
+    normed_moe = rms_scale(total, norm_moe[...][None]).astype(BF16)
+    send_rows[...] = dot(placing[...], normed_moe).astype(BF16)
 
     def row_copy(to_z, to_y):
         to = to_z * dp_n + to_y
@@ -289,8 +300,8 @@
     lax.fori_loop(0, seq_n, dispatch, 0)
     recv_rows[slab(me), :] = send_rows[slab(me), :]
 
-    logits = dot(normed_moe, router_weight[...])
-    gate_value = jax.nn.sigmoid(jnp.sum(logits * picked_f, axis=1, keepdims=True))
+    logits = dot(normed_moe, router_weight[...], ((1,), (1,)))
+    gate_value = jax.nn.sigmoid(jnp.sum(logits * picked, axis=1, keepdims=True))
 
     for copy in own_copies:
         copy.wait()
@@ -301,23 +312,27 @@
     units = gate_v.shape[2]
     tile = units // 3
 
-    def expert_group(i, carry):
-        source_z = for_peers(i, -1, lambda a, b: row_arrival(a, b).wait_recv())
-        at = pl.ds(pl.multiple_of(source_z * group, group), group)
-        x = recv_rows[at, :]
-        acc = jnp.zeros((group, width), F32)
+    def expert_groups(i, carry):
+        places = []
+        for j in range(2):
+            source_z = for_peers(2 * i + j, -1, lambda a, b: row_arrival(a, b).wait_recv())
+            places.append(pl.ds(pl.multiple_of(source_z * group, group), group))
+        x = jnp.concatenate([recv_rows[at, :] for at in places], axis=0)
         for side in range(2):
             for c in range(units // tile):
                 cols = slice(c * tile, (c + 1) * tile)
                 g = dot(x, gate_v[side, :, cols])
                 u = dot(x, up_v[side, :, cols])
-                hidden = (g * jax.nn.sigmoid(g) * u).astype(BF16)
-                acc = acc + dot(hidden, down_v[side, cols, :])
-        out_rows[at, :] = acc.astype(BF16)
-        for_peers(i, -1, lambda a, b: back_copy(a, b).start())
-        return carry
-
-    lax.fori_loop(0, seq_n, expert_group, 0)
+                hidden[:, side * units + c * tile : side * units + (c + 1) * tile] = (
+                    g * jax.nn.sigmoid(g) * u
+                ).astype(BF16)
+        out = dot(hidden[:, :units], down_v[0]) + dot(hidden[:, units:], down_v[1])
+        for j, at in enumerate(places):
+            out_rows[at, :] = out[j * group : (j + 1) * group].astype(BF16)
+            for_peers(2 * i + j, -1, lambda a, b: back_copy(a, b).start())
+        return carry
+
+    lax.fori_loop(0, seq_n // 2, expert_groups, 0)
     back_rows[slab(me), :] = out_rows[slab(me), :]
 
     def await_back(i, carry):
@@ -357,7 +372,7 @@
 ):
     seq_n, head_n, dp_n = lax.axis_size("seq"), lax.axis_size("head"), lax.axis_size("dp")
     tokens, width = series.shape[1:]
-    assert head_n == 2 and tokens == BLOCK and seq_n > 1
+    assert head_n == 2 and tokens == BLOCK and seq_n % 2 == 0
     rows = tokens // 2
     experts = router_weight.shape[1]
     peers = seq_n * dp_n
@@ -389,6 +404,8 @@
             pltpu.VMEM((rows, width), F32),
             pltpu.VMEM((rows, width), F32),
             pltpu.VMEM((rows, slots), BF16),
+            pltpu.VMEM((slots, rows), BF16),
+            pltpu.VMEM((2 * dp_n * cap, 2 * units), BF16),
             pltpu.VMEM((slots, width), BF16),
             pltpu.VMEM((slots, width), BF16),
             pltpu.VMEM((slots, width), BF16),
@@ -411,12 +428,12 @@
         name="layer",
     )(
         series[0],
-        norm_attn[None],
-        qkv_weight.reshape(width, 3 * local),
+        norm_attn,
+        jnp.transpose(qkv_weight, (1, 0, 2)),
         out_weight,
-        norm_moe[None],
-        router_weight,
-        expert_ids[0],
+        norm_moe,
+        router_weight.T,
+        expert_ids.reshape(1, rows),
         gate_weight,
         up_weight,
         down_weight,

time: 73.2 us -> 64.3 us (0.88)
  local copies, waits for them, and re-layouts: 9.46 us -> 1.77 us
  Pallas kernels: 63.4 us -> 62.4 us
    unnamed x11 -> x1, local copies, waits for them, and re-layouts: 5.23 us -> 1.77 us
    reshape x1 -> x0, local copies, waits for them, and re-layouts: 2.25 us -> none  [on_device(): qkv_weight.reshape(width, 3 * local)]
    broadcast_in_dim x2 -> x0, local copies, waits for them, and re-layouts: 1.18 us -> none  [the longest x1 0.6 us: on_device(): norm_attn[None]]
    pallas_call x1, Pallas kernels: 63.4 us -> 62.4 us  [on_device(): pl.pallas_call(functools.partial(layer_kernel, seq_n, dp_n, cap), out_sha...]
    squeeze x1 -> x0, local copies, waits for them, and re-layouts: 0.79 us -> none  [on_device(): expert_ids[0]]
where the time goes in v2:
time: 64.3 us; the launch traced here: 64.2 us
  Pallas kernels  62.4 us (97%)
  local copies, waits for them, and re-layouts  1.77 us (3%)
    pallas_call x1, Pallas kernels, on_device(): pl.pallas_call(functools.partial(layer_kernel, seq_n, dp_n, cap), out_sha...  62.4 us
    unnamed x1, local copies, waits for them, and re-layouts  1.77 us

profile of v2, /device:TPU:0, one launch (start us, length us, event | category | flops | bytes accessed | tf_op | source)
XLA Modules:
  0.0 64.2 jit_solution(16841746467500945036)
XLA Ops:
  0.0 62.4 %layer.1 = bf16[256,768]{1,0:T(8,128)(2,1)} custom-call(bf16[512,768]{1,0:T(8,128)(2,1)} %bitcast.7, f32[768]{0:T(1024)} %norm_attn.1, bf16[3,768,384]{2,1,0:T(8,128)(2,1)} %bitcast.5, bf16[384,768]{1,0:T(8,128)(2,1)} %out_weight.1, f32[768]{0:T(1024)} %norm_moe.1, bf16[16,768]{1,0:T(8,128)(2,1)} %bitcast.8, s32[1,256]{1,0:T(1,128)} %bitcast.9, ...), custom_call_target="tpu_custom_call" | custom-call | tf_op jit(solution)/shard_map/layer/pallas_call | solution.py:388
  62.4 1.8 %copy.12 = bf16[1,256,768]{2,1,0:T(8,128)(2,1)} copy(bf16[1,256,768]{2,1,0:T(8,128)(2,1)} %bitcast.6) | data formatting | bytes 786432

commit v3 on v2

--- a/solution.py
+++ b/solution.py
@@ -47,8 +47,9 @@
     state_in,
     before,
     inside,
-    partial_out,
-    partial_in,
+    mixed_out,
+    mixed_in,
+    out_far,
     residual,
     routing,
     placing,
@@ -114,6 +115,16 @@
 
     lax.fori_loop(0, seq_n, greet, 0)
 
+    def core_copy(src, dst, j):
+        return pltpu.make_async_remote_copy(
+            src_ref=src,
+            dst_ref=dst,
+            send_sem=r_send.at[j],
+            recv_sem=r_recv.at[j],
+            device_id={"head": other},
+            device_id_type=MESH,
+        )
+
     weights = ((gate_hbm, gate_v), (up_hbm, up_v), (down_hbm, down_v))
     own_copies = [
         pltpu.make_async_copy(src.at[0], dst.at[0], own_sem.at[j])
@@ -159,6 +170,8 @@
         return carry
 
     lax.fori_loop(0, seq_n - 1 - z, send_state, 0)
+    out_copy = core_copy(out_weight, out_far, 1)
+    out_copy.start()
     far_copies[0].start()
     far_copies[1].start()
 
@@ -217,7 +230,7 @@
     state_hi = before[...].astype(BF16)
     state_lo = (before[...] - state_hi.astype(F32)).astype(BF16)
 
-    def project_out(which):
+    def mix(which):
         start = pl.multiple_of(which * half, half)
         at = pl.ds(start, half)
         position = z * tokens + start + 1 + lax.broadcasted_iota(jnp.int32, (half, 1), 0)
@@ -228,23 +241,17 @@
             q = projected[at, cols]
             carried = dot(q, state_hi[cols]) + dot(q, state_lo[cols])
             mixed.append(((inside[at, cols] + carried) * scale).astype(BF16))
-        return dot(jnp.concatenate(mixed, axis=1), out_weight[...])
-
-    partial_out[...] = project_out(other)
-    sum_copy = pltpu.make_async_remote_copy(
-        src_ref=partial_out,
-        dst_ref=partial_in,
-        send_sem=r_send,
-        recv_sem=r_recv,
-        device_id={"head": other},
-        device_id_type=MESH,
-    )
-    sum_copy.start()
+        return jnp.concatenate(mixed, axis=1)
+
+    mixed_out[...] = mix(other)
+    mixed_copy = core_copy(mixed_out, mixed_in, 0)
+    mixed_copy.start()
     far_copies[2].start()
     own_at = pl.ds(pl.multiple_of(head * half, half), half)
-    residual[...] = project_out(head) + series[own_at, :].astype(F32)
-    sum_copy.wait_recv()
-    total = residual[...] + partial_in[...]
+    residual[...] = dot(mix(head), out_weight[...]) + series[own_at, :].astype(F32)
+    out_copy.wait_recv()
+    mixed_copy.wait_recv()
+    total = residual[...] + dot(mixed_in[...], out_far[...])
     residual[...] = total
     normed_moe = rms_scale(total, norm_moe[...][None]).astype(BF16)
     send_rows[...] = dot(placing[...], normed_moe).astype(BF16)
@@ -293,11 +300,11 @@
             device_id_type=MESH,
         )
 
-    def dispatch(i, carry):
-        for_peers(i, 1, lambda a, b: row_copy(a, b).start())
-        return carry
-
-    lax.fori_loop(0, seq_n, dispatch, 0)
+    def dispatch(i):
+        for j in range(2):
+            for_peers(2 * i + j, 1, lambda a, b: row_copy(a, b).start())
+
+    dispatch(0)
     recv_rows[slab(me), :] = send_rows[slab(me), :]
 
     logits = dot(normed_moe, router_weight[...], ((1,), (1,)))
@@ -313,6 +320,13 @@
     tile = units // 3
 
     def expert_groups(i, carry):
+        for j in range(2):
+            for_peers(2 * i + j, 1, lambda a, b: row_copy(a, b).wait_send())
+
+        @pl.when(i + 1 < seq_n // 2)
+        def _():
+            dispatch(i + 1)
+
         places = []
         for j in range(2):
             source_z = for_peers(2 * i + j, -1, lambda a, b: row_arrival(a, b).wait_recv())
@@ -344,7 +358,6 @@
     layer_out[...] = (residual[...] + gate_value * routed).astype(BF16)
 
     def sent_rows(i, carry):
-        for_peers(i, 1, lambda a, b: row_copy(a, b).wait_send())
         for_peers(i, -1, lambda a, b: back_copy(a, b).wait_send())
         return carry
 
@@ -355,7 +368,8 @@
         return carry
 
     lax.fori_loop(0, seq_n - 1 - z, sent_state, 0)
-    sum_copy.wait_send()
+    mixed_copy.wait_send()
+    out_copy.wait_send()
 
 
 def on_device(
@@ -400,8 +414,9 @@
             pltpu.VMEM((seq_n, local, HD), BF16),
             pltpu.VMEM((local, HD), F32),
             pltpu.VMEM((tokens, local), F32),
-            pltpu.VMEM((rows, width), F32),
-            pltpu.VMEM((rows, width), F32),
+            pltpu.VMEM((rows, local), BF16),
+            pltpu.VMEM((rows, local), BF16),
+            pltpu.VMEM((local, width), BF16),
             pltpu.VMEM((rows, width), F32),
             pltpu.VMEM((rows, slots), BF16),
             pltpu.VMEM((slots, rows), BF16),
@@ -415,15 +430,15 @@
             dma((3,)),
             dma((seq_n,)),
             dma((seq_n,)),
-            dma,
-            dma,
+            dma((2,)),
+            dma((2,)),
             dma((peers,)),
             dma((peers,)),
             dma((peers,)),
             dma((peers,)),
         ],
         compiler_params=pltpu.CompilerParams(
-            collective_id=0, has_side_effects=True, vmem_limit_bytes=56 * 1024 * 1024
+            collective_id=0, has_side_effects=True, vmem_limit_bytes=44 * 1024 * 1024
         ),
         name="layer",
     )(

time: 64.3 us -> 68.1 us (1.059); the launches traced: 64.2 us -> 67 us
  local copies, waits for them, and re-layouts: 1.77 us -> 10.5 us
  Pallas kernels: 62.4 us -> 56.4 us
    unnamed x1 -> x19, local copies, waits for them, and re-layouts: 1.77 us -> 10.5 us
    pallas_call x1, Pallas kernels: 62.4 us -> 56.4 us  [on_device(): pl.pallas_call(functools.partial(layer_kernel, seq_n, dp_n, cap), out_sha...]
where the time goes in v3:
time: 68.1 us; the launch traced here: 67 us
  Pallas kernels  56.4 us (83%)
  local copies, waits for them, and re-layouts  10.5 us (15%)
    pallas_call x1, Pallas kernels, on_device(): pl.pallas_call(functools.partial(layer_kernel, seq_n, dp_n, cap), out_sha...  56.4 us
    unnamed x19, local copies, waits for them, and re-layouts  10.5 us

profile of v3, /device:TPU:0, one launch (start us, length us, event | category | flops | bytes accessed | tf_op | source)
XLA Modules:
  0.0 67.0 jit_solution(16441636736013014457)
XLA Ops:
  0.0 0.0 copy-start
  0.0 1.7 %copy-done = bf16[1,768,1536]{2,1,0:T(8,128)(2,1)S(1)} copy-done((bf16[1,768,1536]{2,1,0:T(8,128)(2,1)S(1)}, bf16[1,768,1536]{2,1,0:T(8,128)(2,1)}, u32[]{:S(2)}) %copy-start) | copy-done | bytes 2359320
  1.7 0.0 copy-start.1
  1.7 1.7 %copy-done.1 = bf16[1,768,1536]{2,1,0:T(8,128)(2,1)S(1)} copy-done((bf16[1,768,1536]{2,1,0:T(8,128)(2,1)S(1)}, bf16[1,768,1536]{2,1,0:T(8,128)(2,1)}, u32[]{:S(2)}) %copy-start.1) | copy-done | bytes 2359320
  3.3 0.0 copy-start.2
  3.3 1.5 %copy-done.2 = bf16[768,3,384]{2,0,1:T(8,128)(2,1)S(1)} copy-done((bf16[768,3,384]{2,0,1:T(8,128)(2,1)S(1)}, bf16[768,3,384]{2,0,1:T(8,128)(2,1)}, u32[]{:S(2)}) %copy-start.2) | copy-done | bytes 1769496
  4.8 0.0 copy-start.3
  4.8 1.1 %copy-done.3 = bf16[1,512,768]{2,1,0:T(8,128)(2,1)S(1)} copy-done((bf16[1,512,768]{2,1,0:T(8,128)(2,1)S(1)}, bf16[1,512,768]{2,1,0:T(8,128)(2,1)}, u32[]{:S(2)}) %copy-start.3) | copy-done | bytes 786456
  5.9 0.0 copy-start.4
  5.9 1.1 %copy-done.4 = bf16[384,768]{1,0:T(8,128)(2,1)S(1)} copy-done((bf16[384,768]{1,0:T(8,128)(2,1)S(1)}, bf16[384,768]{1,0:T(8,128)(2,1)}, u32[]{:S(2)}) %copy-start.4) | copy-done | bytes 589848
  7.0 0.0 copy-start.5
  7.0 0.7 %copy-done.5 = bf16[768,16]{0,1:T(8,128)(2,1)S(1)} copy-done((bf16[768,16]{0,1:T(8,128)(2,1)S(1)}, bf16[768,16]{0,1:T(8,128)(2,1)}, u32[]{:S(2)}) %copy-start.5) | copy-done | bytes 24600
  7.7 0.0 copy-start.6
  7.7 0.7 %copy-done.6 = f32[768]{0:T(1024)S(1)} copy-done((f32[768]{0:T(1024)S(1)}, f32[768]{0:T(1024)}, u32[]{:S(2)}) %copy-start.6) | copy-done | bytes 3096
  8.4 0.0 copy-start.7
  8.4 0.7 %copy-done.7 = f32[768]{0:T(1024)S(1)} copy-done((f32[768]{0:T(1024)S(1)}, f32[768]{0:T(1024)}, u32[]{:S(2)}) %copy-start.7) | copy-done | bytes 3096
  9.1 0.0 copy-start.8
  9.1 0.7 %copy-done.8 = s32[1,256,1]{1,2,0:T(1,128)S(1)} copy-done((s32[1,256,1]{1,2,0:T(1,128)S(1)}, s32[1,256,1]{1,2,0:T(1,128)}, u32[]{:S(2)}) %copy-start.8) | copy-done | bytes 1048
  9.8 56.4 %layer.1 = bf16[256,768]{1,0:T(8,128)(2,1)S(1)} custom-call(bf16[512,768]{1,0:T(8,128)(2,1)S(1)} %bitcast.7, f32[768]{0:T(1024)S(1)} %copy-done.6, bf16[3,768,384]{2,1,0:T(8,128)(2,1)S(1)} %bitcast.5, bf16[384,768]{1,0:T(8,128)(2,1)S(1)} %copy-done.4, f32[768]{0:T(1024)S(1)} %copy-done.7, bf16[16,768]{1,0:T(8,128)(2,1)S(1)} %bitcast.8, ...), custom_call_target="tpu_custom_call" | custom-call | tf_op jit(solution)/shard_map/layer/pallas_call | solution.py:402
  66.2 0.7 %copy.12 = bf16[1,256,768]{2,1,0:T(8,128)(2,1)} copy(bf16[1,256,768]{2,1,0:T(8,128)(2,1)S(1)} %bitcast.6) | data formatting | bytes 786432
Async XLA Ops:
  0.0 1.7 %copy-start = (bf16[1,768,1536]{2,1,0:T(8,128)(2,1)S(1)}, bf16[1,768,1536]{2,1,0:T(8,128)(2,1)}, u32[]{:S(2)}) copy-start(bf16[1,768,1536]{2,1,0:T(8,128)(2,1)} %gate_hbm.1) | copy-start | bytes 7077892
  1.7 1.7 %copy-start.1 = (bf16[1,768,1536]{2,1,0:T(8,128)(2,1)S(1)}, bf16[1,768,1536]{2,1,0:T(8,128)(2,1)}, u32[]{:S(2)}) copy-start(bf16[1,768,1536]{2,1,0:T(8,128)(2,1)} %up_hbm.1) | copy-start | bytes 7077892
  3.3 1.5 %copy-start.2 = (bf16[768,3,384]{2,0,1:T(8,128)(2,1)S(1)}, bf16[768,3,384]{2,0,1:T(8,128)(2,1)}, u32[]{:S(2)}) copy-start(bf16[768,3,384]{2,0,1:T(8,128)(2,1)} %param.12) | copy-start | bytes 5308420
  4.8 1.1 %copy-start.3 = (bf16[1,512,768]{2,1,0:T(8,128)(2,1)S(1)}, bf16[1,512,768]{2,1,0:T(8,128)(2,1)}, u32[]{:S(2)}) copy-start(bf16[1,512,768]{2,1,0:T(8,128)(2,1)} %param.10) | copy-start | bytes 2359300
  5.9 1.1 %copy-start.4 = (bf16[384,768]{1,0:T(8,128)(2,1)S(1)}, bf16[384,768]{1,0:T(8,128)(2,1)}, u32[]{:S(2)}) copy-start(bf16[384,768]{1,0:T(8,128)(2,1)} %out_weight.1) | copy-start | bytes 1769476
  7.0 0.7 %copy-start.5 = (bf16[768,16]{0,1:T(8,128)(2,1)S(1)}, bf16[768,16]{0,1:T(8,128)(2,1)}, u32[]{:S(2)}) copy-start(bf16[768,16]{0,1:T(8,128)(2,1)} %param.15) | copy-start | bytes 73732
  7.7 0.7 %copy-start.6 = (f32[768]{0:T(1024)S(1)}, f32[768]{0:T(1024)}, u32[]{:S(2)}) copy-start(f32[768]{0:T(1024)} %norm_attn.1) | copy-start | bytes 9220
  8.4 0.7 %copy-start.7 = (f32[768]{0:T(1024)S(1)}, f32[768]{0:T(1024)}, u32[]{:S(2)}) copy-start(f32[768]{0:T(1024)} %norm_moe.1) | copy-start | bytes 9220
  9.1 0.7 %copy-start.8 = (s32[1,256,1]{1,2,0:T(1,128)S(1)}, s32[1,256,1]{1,2,0:T(1,128)}, u32[]{:S(2)}) copy-start(s32[1,256,1]{1,2,0:T(1,128)} %param.16) | copy-start | bytes 3076

commit v4 on v3

--- a/solution.py
+++ b/solution.py
@@ -27,6 +27,17 @@
     seq_n,
     dp_n,
     cap,
+    series_hbm,
+    norm_attn_hbm,
+    qkv_hbm,
+    out_hbm,
+    norm_moe_hbm,
+    router_hbm,
+    ids_hbm,
+    gate_hbm,
+    up_hbm,
+    down_hbm,
+    layer_out,
     series,
     norm_attn,
     qkv_weight,
@@ -34,10 +45,6 @@
     norm_moe,
     router_weight,
     expert_ids,
-    gate_hbm,
-    up_hbm,
-    down_hbm,
-    layer_out,
     gate_v,
     up_v,
     down_v,
@@ -58,6 +65,7 @@
     recv_rows,
     out_rows,
     back_rows,
+    in_sem,
     own_sem,
     w_send,
     w_recv,
@@ -100,6 +108,25 @@
     def slab(expert):
         return pl.ds(pl.multiple_of(expert * cap, cap), cap)
 
+    fetches = [
+        pltpu.make_async_copy(src, dst, in_sem.at[j])
+        for j, (src, dst) in enumerate(
+            (
+                (series_hbm, series),
+                (norm_attn_hbm, norm_attn),
+                (qkv_hbm.at[1], qkv_weight.at[1]),
+                (qkv_hbm.at[2], qkv_weight.at[2]),
+                (qkv_hbm.at[0], qkv_weight.at[0]),
+                (ids_hbm, expert_ids),
+                (out_hbm, out_weight),
+                (norm_moe_hbm, norm_moe),
+                (router_hbm, router_weight),
+            )
+        )
+    ]
+    for fetch in fetches:
+        fetch.start()
+
     barrier = pltpu.get_barrier_semaphore()
     pl.semaphore_signal(barrier, inc=1, device_id={"head": other}, device_id_type=MESH)
 
@@ -141,11 +168,11 @@
         )
         for j, (src, dst) in enumerate(weights)
     ]
-    for copy in own_copies:
-        copy.start()
-
+    fetches[0].wait()
+    fetches[1].wait()
     normed[...] = rms_scale(series[...].astype(F32), norm_attn[...][None]).astype(BF16)
     for j in (1, 2):
+        fetches[1 + j].wait()
         projected[:, j * local : (j + 1) * local] = dot(normed[...], qkv_weight[j]).astype(BF16)
     for h in range(heads):
         at = pl.ds(h * HD, HD)
@@ -170,8 +197,12 @@
         return carry
 
     lax.fori_loop(0, seq_n - 1 - z, send_state, 0)
+    for fetch in fetches[4:]:
+        fetch.wait()
     out_copy = core_copy(out_weight, out_far, 1)
     out_copy.start()
+    for copy in own_copies:
+        copy.start()
     far_copies[0].start()
     far_copies[1].start()
 
@@ -397,14 +428,21 @@
     cap = -(-capacity // 16) * 16
     slots = experts * cap
     vmem = pl.BlockSpec(memory_space=pltpu.VMEM)
-    hbm = pl.BlockSpec(memory_space=pl.ANY)
+    hbm = pl.BlockSpec(memory_space=pltpu.HBM)
     dma = pltpu.SemaphoreType.DMA
     out = pl.pallas_call(
         functools.partial(layer_kernel, seq_n, dp_n, cap),
         out_shape=jax.ShapeDtypeStruct((rows, width), BF16),
-        in_specs=[vmem] * 7 + [hbm] * 3,
+        in_specs=[hbm] * 10,
         out_specs=vmem,
         scratch_shapes=[
+            pltpu.VMEM((tokens, width), BF16),
+            pltpu.VMEM((width,), F32),
+            pltpu.VMEM((3, width, local), BF16),
+            pltpu.VMEM((local, width), BF16),
+            pltpu.VMEM((width,), F32),
+            pltpu.VMEM((experts, width), BF16),
+            pltpu.VMEM((1, rows), jnp.int32),
             pltpu.VMEM((2, width, units), BF16),
             pltpu.VMEM((2, width, units), BF16),
             pltpu.VMEM((2, units, width), BF16),
@@ -425,6 +463,7 @@
             pltpu.VMEM((slots, width), BF16),
             pltpu.VMEM((slots, width), BF16),
             pltpu.VMEM((slots, width), BF16),
+            dma((9,)),
             dma((3,)),
             dma((3,)),
             dma((3,)),
@@ -442,16 +481,21 @@
         ),
         name="layer",
     )(
-        series[0],
-        norm_attn,
-        jnp.transpose(qkv_weight, (1, 0, 2)),
-        out_weight,
-        norm_moe,
-        router_weight.T,
-        expert_ids.reshape(1, rows),
-        gate_weight,
-        up_weight,
-        down_weight,
+        *[
+            pltpu.with_memory_space_constraint(operand, pltpu.HBM)
+            for operand in (
+                series[0],
+                norm_attn,
+                jnp.transpose(qkv_weight, (1, 0, 2)),
+                out_weight,
+                norm_moe,
+                router_weight.T,
+                expert_ids.reshape(1, rows),
+                gate_weight,
+                up_weight,
+                down_weight,
+            )
+        ]
     )
     return out[None]
 

time: 68.1 us -> 59.2 us (0.87); the launches traced: 67 us -> 59 us
  local copies, waits for them, and re-layouts: 10.5 us -> 0.75 us
  Pallas kernels: 56.4 us -> 58.2 us
    unnamed x19 -> x1, local copies, waits for them, and re-layouts: 10.5 us -> 0.75 us
    pallas_call x1, Pallas kernels: 56.4 us -> 58.2 us  [on_device(): pl.pallas_call(functools.partial(layer_kernel, seq_n, dp_n, cap), out_sha...]
where the time goes in v4:
time: 59.2 us; the launch traced here: 59 us
  Pallas kernels  58.2 us (98%)
  local copies, waits for them, and re-layouts  0.75 us (1%)
    pallas_call x1, Pallas kernels, on_device(): pl.pallas_call(functools.partial(layer_kernel, seq_n, dp_n, cap), out_sha...  58.2 us

profile of v4, /device:TPU:0, one launch (start us, length us, event | category | flops | bytes accessed | tf_op | source)
XLA Modules:
  0.0 59.0 jit_solution(8773159079291985454)
XLA Ops:
  0.0 58.2 %layer.1 = bf16[256,768]{1,0:T(8,128)(2,1)S(1)} custom-call(bf16[512,768]{1,0:T(8,128)(2,1)} %bitcast.7, f32[768]{0:T(1024)} %norm_attn_hbm.1, bf16[3,768,384]{2,1,0:T(8,128)(2,1)} %bitcast.6, bf16[384,768]{1,0:T(8,128)(2,1)} %out_hbm.1, f32[768]{0:T(1024)} %norm_moe_hbm.1, bf16[16,768]{1,0:T(8,128)(2,1)} %bitcast.8, s32[1,256]{1,0:T(1,128)} %bitcast.9, ...), custom_call_target="tpu_custom_call" | custom-call | tf_op jit(solution)/shard_map/layer/pallas_call | solution.py:433
  58.2 0.7 %copy.12 = bf16[1,256,768]{2,1,0:T(8,128)(2,1)} copy(bf16[1,256,768]{2,1,0:T(8,128)(2,1)S(1)} %bitcast.5) | data formatting | bytes 786432

commit v5 on v4

--- a/solution.py
+++ b/solution.py
@@ -350,19 +350,19 @@
     units = gate_v.shape[2]
     tile = units // 3
 
-    def expert_groups(i, carry):
-        for j in range(2):
-            for_peers(2 * i + j, 1, lambda a, b: row_copy(a, b).wait_send())
-
-        @pl.when(i + 1 < seq_n // 2)
+    def expert_group(i, carry):
+        @pl.when(i % 2 == 1)
         def _():
-            dispatch(i + 1)
-
-        places = []
-        for j in range(2):
-            source_z = for_peers(2 * i + j, -1, lambda a, b: row_arrival(a, b).wait_recv())
-            places.append(pl.ds(pl.multiple_of(source_z * group, group), group))
-        x = jnp.concatenate([recv_rows[at, :] for at in places], axis=0)
+            for j in range(2):
+                for_peers(i - 1 + j, 1, lambda a, b: row_copy(a, b).wait_send())
+
+            @pl.when(i + 1 < seq_n)
+            def _():
+                dispatch((i + 1) // 2)
+
+        source_z = for_peers(i, -1, lambda a, b: row_arrival(a, b).wait_recv())
+        at = pl.ds(pl.multiple_of(source_z * group, group), group)
+        x = recv_rows[at, :]
         for side in range(2):
             for c in range(units // tile):
                 cols = slice(c * tile, (c + 1) * tile)
@@ -372,12 +372,11 @@
                     g * jax.nn.sigmoid(g) * u
                 ).astype(BF16)
         out = dot(hidden[:, :units], down_v[0]) + dot(hidden[:, units:], down_v[1])
-        for j, at in enumerate(places):
-            out_rows[at, :] = out[j * group : (j + 1) * group].astype(BF16)
-            for_peers(2 * i + j, -1, lambda a, b: back_copy(a, b).start())
-        return carry
-
-    lax.fori_loop(0, seq_n // 2, expert_groups, 0)
+        out_rows[at, :] = out.astype(BF16)
+        for_peers(i, -1, lambda a, b: back_copy(a, b).start())
+        return carry
+
+    lax.fori_loop(0, seq_n, expert_group, 0)
     back_rows[slab(me), :] = out_rows[slab(me), :]
 
     def await_back(i, carry):
@@ -458,7 +457,7 @@
             pltpu.VMEM((rows, width), F32),
             pltpu.VMEM((rows, slots), BF16),
             pltpu.VMEM((slots, rows), BF16),
-            pltpu.VMEM((2 * dp_n * cap, 2 * units), BF16),
+            pltpu.VMEM((dp_n * cap, 2 * units), BF16),
             pltpu.VMEM((slots, width), BF16),
             pltpu.VMEM((slots, width), BF16),
             pltpu.VMEM((slots, width), BF16),

time: 59.2 us -> 62.8 us (1.061)
  Pallas kernels: 58.2 us -> 61.9 us
    pallas_call x1, Pallas kernels: 58.2 us -> 61.9 us  [on_device(): pl.pallas_call(functools.partial(layer_kernel, seq_n, dp_n, cap), out_sha...]
where the time goes in v5:
time: 62.8 us; the launch traced here: 62.7 us
  Pallas kernels  61.9 us (99%)
  local copies, waits for them, and re-layouts  0.75 us (1%)
    pallas_call x1, Pallas kernels, on_device(): pl.pallas_call(functools.partial(layer_kernel, seq_n, dp_n, cap), out_sha...  61.9 us

profile of v5, /device:TPU:0, one launch (start us, length us, event | category | flops | bytes accessed | tf_op | source)
XLA Modules:
  0.0 62.7 jit_solution(6367748855223621555)
XLA Ops:
  0.0 61.9 %layer.1 = bf16[256,768]{1,0:T(8,128)(2,1)S(1)} custom-call(bf16[512,768]{1,0:T(8,128)(2,1)} %bitcast.7, f32[768]{0:T(1024)} %norm_attn_hbm.1, bf16[3,768,384]{2,1,0:T(8,128)(2,1)} %bitcast.6, bf16[384,768]{1,0:T(8,128)(2,1)} %out_hbm.1, f32[768]{0:T(1024)} %norm_moe_hbm.1, bf16[16,768]{1,0:T(8,128)(2,1)} %bitcast.8, s32[1,256]{1,0:T(1,128)} %bitcast.9, ...), custom_call_target="tpu_custom_call" | custom-call | tf_op jit(solution)/shard_map/layer/pallas_call | solution.py:432
  61.9 0.7 %copy.12 = bf16[1,256,768]{2,1,0:T(8,128)(2,1)} copy(bf16[1,256,768]{2,1,0:T(8,128)(2,1)S(1)} %bitcast.5) | data formatting | bytes 786432

commit v6 on v4

--- a/solution.py
+++ b/solution.py
@@ -50,6 +50,7 @@
     down_v,
     normed,
     projected,
+    state_sum,
     state_own,
     state_in,
     before,
@@ -178,25 +179,29 @@
         at = pl.ds(h * HD, HD)
         keys = projected[:, local + h * HD : local + (h + 1) * HD]
         values = projected[:, 2 * local + h * HD : 2 * local + (h + 1) * HD]
-        state_own[at, :] = dot(keys, values, ((0,), (0,))).astype(BF16)
+        state_sum[at, :] = dot(keys, values, ((0,), (0,)))
 
     pl.semaphore_wait(barrier, seq_n * dp_n)
 
-    def state_copy(to):
+    def state_copy(source, to, h):
+        at = pl.ds(h * HD, HD)
         return pltpu.make_async_remote_copy(
-            src_ref=state_own,
-            dst_ref=state_in.at[z],
-            send_sem=s_send.at[to],
-            recv_sem=s_recv.at[z],
+            src_ref=state_own.at[at],
+            dst_ref=state_in.at[source, at],
+            send_sem=s_send.at[to, h],
+            recv_sem=s_recv.at[source, h],
             device_id={"seq": to},
             device_id_type=MESH,
         )
 
-    def send_state(j, carry):
-        state_copy(seq_n - 1 - j).start()
-        return carry
-
-    lax.fori_loop(0, seq_n - 1 - z, send_state, 0)
+    odd = z % 2
+
+    @pl.when(odd == 0)
+    def _():
+        state_own[...] = state_sum[...].astype(BF16)
+        for h in range(heads):
+            state_copy(z, z + 1, h).start()
+
     for fetch in fetches[4:]:
         fetch.wait()
     out_copy = core_copy(out_weight, out_far, 1)
@@ -207,6 +212,21 @@
     far_copies[1].start()
 
     projected[:, :local] = dot(normed[...], qkv_weight[0]).astype(BF16)
+
+    @pl.when(odd == 1)
+    def _():
+        for h in range(heads):
+            at = pl.ds(h * HD, HD)
+            state_copy(z - 1, z - 1, h).wait_recv()
+            pair = state_sum[at, :] + state_in[z - 1, at, :].astype(F32)
+            state_own[at, :] = pair.astype(BF16)
+
+            def send_pair(j, carry):
+                state_copy(z, seq_n - 1 - j, h).start()
+                return carry
+
+            lax.fori_loop(0, seq_n - 1 - z, send_pair, 0)
+
     for h in range(heads):
         cols = slice(h * HD, (h + 1) * HD)
         for part in range(2):
@@ -244,19 +264,18 @@
 
     before[...] = jnp.zeros_like(before)
 
-    def add_state(j, carry):
-        pltpu.make_async_remote_copy(
-            src_ref=state_own,
-            dst_ref=state_in.at[j],
-            send_sem=s_send.at[j],
-            recv_sem=s_recv.at[j],
-            device_id={"seq": j},
-            device_id_type=MESH,
-        ).wait_recv()
-        before[...] += state_in[j].astype(F32)
+    @pl.when(odd == 1)
+    def _():
+        before[...] = state_in[z - 1].astype(F32)
+
+    def add_pair(j, carry):
+        source = 2 * j + 1
+        for h in range(heads):
+            state_copy(source, source, h).wait_recv()
+        before[...] += state_in[source].astype(F32)
         return carry
 
-    lax.fori_loop(0, z, add_state, 0)
+    lax.fori_loop(0, z // 2, add_pair, 0)
 
     state_hi = before[...].astype(BF16)
     state_lo = (before[...] - state_hi.astype(F32)).astype(BF16)
@@ -394,11 +413,20 @@
 
     lax.fori_loop(0, seq_n, sent_rows, 0)
 
-    def sent_state(j, carry):
-        state_copy(seq_n - 1 - j).wait_send()
-        return carry
-
-    lax.fori_loop(0, seq_n - 1 - z, sent_state, 0)
+    @pl.when(odd == 0)
+    def _():
+        for h in range(heads):
+            state_copy(z, z + 1, h).wait_send()
+
+    @pl.when(odd == 1)
+    def _():
+        def sent_pair(j, carry):
+            for h in range(heads):
+                state_copy(z, seq_n - 1 - j, h).wait_send()
+            return carry
+
+        lax.fori_loop(0, seq_n - 1 - z, sent_pair, 0)
+
     mixed_copy.wait_send()
     out_copy.wait_send()
 
@@ -448,6 +476,7 @@
             pltpu.VMEM((2, units, width), BF16),
             pltpu.VMEM((tokens, width), BF16),
             pltpu.VMEM((tokens, 3 * local), BF16),
+            pltpu.VMEM((local, HD), F32),
             pltpu.VMEM((local, HD), BF16),
             pltpu.VMEM((seq_n, local, HD), BF16),
             pltpu.VMEM((local, HD), F32),
@@ -467,8 +496,8 @@
             dma((3,)),
             dma((3,)),
             dma((3,)),
-            dma((seq_n,)),
-            dma((seq_n,)),
+            dma((seq_n, local // HD)),
+            dma((seq_n, local // HD)),
             dma((2,)),
             dma((2,)),
             dma((peers,)),

time: 59.2 us -> 59 us (level)
  no operation moved by 1% of the time
where the time goes in v6:
time: 59 us; the launch traced here: 58.9 us
  Pallas kernels  58.1 us (98%)
  local copies, waits for them, and re-layouts  0.75 us (1%)
    pallas_call x1, Pallas kernels, on_device(): pl.pallas_call(functools.partial(layer_kernel, seq_n, dp_n, cap), out_sha...  58.1 us

profile of v6, /device:TPU:0, one launch (start us, length us, event | category | flops | bytes accessed | tf_op | source)
XLA Modules:
  0.0 58.9 jit_solution(3750747046192166463)
XLA Ops:
  0.0 58.1 %layer.1 = bf16[256,768]{1,0:T(8,128)(2,1)S(1)} custom-call(bf16[512,768]{1,0:T(8,128)(2,1)} %bitcast.7, f32[768]{0:T(1024)} %norm_attn_hbm.1, bf16[3,768,384]{2,1,0:T(8,128)(2,1)} %bitcast.6, bf16[384,768]{1,0:T(8,128)(2,1)} %out_hbm.1, f32[768]{0:T(1024)} %norm_moe_hbm.1, bf16[16,768]{1,0:T(8,128)(2,1)} %bitcast.8, s32[1,256]{1,0:T(1,128)} %bitcast.9, ...), custom_call_target="tpu_custom_call" | custom-call | tf_op jit(solution)/shard_map/layer/pallas_call | solution.py:461
  58.2 0.7 %copy.12 = bf16[1,256,768]{2,1,0:T(8,128)(2,1)} copy(bf16[1,256,768]{2,1,0:T(8,128)(2,1)S(1)} %bitcast.5) | data formatting | bytes 786432
